TPU v7x, 32 devices: a whole 2x2x4 slice. The times are simulated.
32 devices in a mesh: lat: 4 (over y, x), lon: 8 (over z, core).
Axes of the slice: x: 2, y: 2, z: 4, core: 2. Of those that a mesh axis runs over, the one named last changes fastest.
Arguments:
- probes: float32 [8, 4, 512, 512], P(None, None, 'lon', 'lat'), may hold values from -6 to 6
- wind: float32 [2, 4, 512, 512], P(None, None, 'lon', 'lat'), may hold values from -0.45 to 0.45
- wind_tend: float32 [2, 4, 512, 512], P(None, None, 'lon', 'lat'), may hold values from -0.05 to 0.05
- obs_weight: float32 [4, 512, 512], P(None, 'lon', 'lat'), may hold values from 0.5 to 18
Outputs:
- basis: float32 [8, 4, 512, 512], P(None, None, 'lon', 'lat')
- factor: float32 [8, 8], replicated
All inputs are finite; a program needn't handle non-finite values.
Results may differ from a plain program's by a relative error of at most 0.00012.
Values sent between devices are 32-bit elements; how exact they have to be, the bound alone decides.
A program may use at most 64 MiB of HBM per device.

v0:
```python
import jax
import jax.numpy as jnp
from jax import lax
from jax.sharding import PartitionSpec as P

STEPS = 4


diffuse = 0.24


def padded(cells, sides, width, closed):
    for axis, dim in sides:
        count = lax.axis_size(axis)
        ends = count if closed else count - 1
        head = lax.slice_in_dim(cells, 0, width, axis=dim)
        tail = lax.slice_in_dim(cells, cells.shape[dim] - width, cells.shape[dim], axis=dim)
        cells = jnp.concatenate(
            [
                lax.ppermute(tail, axis, [(i, (i + 1) % count) for i in range(ends)]),
                cells,
                lax.ppermute(head, axis, [((i + 1) % count, i) for i in range(ends)]),
            ],
            axis=dim,
        )
    return cells


def forward_step(field, lon_rate, lat_rate):
    east = lon_rate[..., 1:-1, 1:-1]
    north = lat_rate[..., 1:-1, 1:-1]
    middle = field[..., 1:-1, 1:-1]
    return (
        (1.0 - 4.0 * diffuse) * middle
        + (diffuse - east) * field[..., 2:, 1:-1]
        + (diffuse + east) * field[..., :-2, 1:-1]
        + (diffuse - north) * field[..., 1:-1, 2:]
        + (diffuse + north) * field[..., 1:-1, :-2]
    )


def adjoint_step(field, lon_rate, lat_rate):
    middle = field[..., 1:-1, 1:-1]
    return (
        (1.0 - 4.0 * diffuse) * middle
        + (diffuse - lon_rate[..., :-2, 1:-1]) * field[..., :-2, 1:-1]
        + (diffuse + lon_rate[..., 2:, 1:-1]) * field[..., 2:, 1:-1]
        + (diffuse - lat_rate[..., 1:-1, :-2]) * field[..., 1:-1, :-2]
        + (diffuse + lat_rate[..., 1:-1, 2:]) * field[..., 1:-1, 2:]
    )


def pad_edges(data, depth):
    data = padded(data, (("lon", 2),), depth, True)
    return padded(data, (("lat", 3),), depth, False)


def lower_inverse(lower):
    eye = jnp.eye(lower.shape[0], dtype=lower.dtype)
    return lax.linalg.triangular_solve(lower, eye, left_side=True, lower=True)


def body(probes, wind, wind_tend, obs_weight):
    width_lon = probes.shape[2]
    width_lat = probes.shape[3]
    winds = jnp.concatenate((wind, wind_tend), axis=0)

    def rates(source, margin, step, radius):
        start = margin - radius
        piece = source[
            :, :, start : start + width_lon + 2 * radius, start : start + width_lat + 2 * radius
        ]
        return (0.5 * (piece[0] + step * piece[2]), 0.5 * (piece[1] + step * piece[3]))

    def lat_mask(radius):
        total = width_lat * lax.axis_size("lat")
        index = (
            lax.axis_index("lat") * width_lat
            - radius
            + jnp.arange(width_lat + 2 * radius, dtype=jnp.int32)
        )
        return ((index >= 0) & (index < total)).astype(jnp.float32)

    margin = 2 * STEPS
    stacked = jnp.concatenate((winds, obs_weight[None], probes), axis=0)
    stacked = pad_edges(stacked, margin)
    padded_winds = stacked[:4]
    padded_weight = stacked[4]
    field = stacked[5:]
    radius = margin
    for step in range(STEPS):
        lon_rate, lat_rate = rates(padded_winds, margin, step, radius)
        field = forward_step(field, lon_rate, lat_rate)
        radius = radius - 1
        field = field * lat_mask(radius)
    start = margin - radius
    field = (
        field
        * padded_weight[
            :, start : start + width_lon + 2 * radius, start : start + width_lat + 2 * radius
        ]
    )
    for step in reversed(range(STEPS)):
        lon_rate, lat_rate = rates(padded_winds, margin, step, radius)
        field = adjoint_step(field, lon_rate, lat_rate)
        radius = radius - 1
        field = field * lat_mask(radius)
    high = lax.Precision.HIGHEST
    flat = field.reshape(field.shape[0], -1)
    gram = lax.psum(jnp.einsum("pc,qc->pq", flat, flat, precision=high), ("lat", "lon"))
    lower = jnp.linalg.cholesky(gram)
    result = jnp.dot(lower_inverse(lower), flat, precision=high)
    upper = lower.T
    cells = field.shape[1] * width_lon * width_lat * lax.axis_size("lat") * lax.axis_size("lon")
    scale = jnp.sqrt(jnp.float32(cells))
    return ((result * scale).reshape(field.shape), upper / scale)


def solution(mesh):
    placed = (
        P(None, None, "lon", "lat"),
        P(None, None, "lon", "lat"),
        P(None, None, "lon", "lat"),
        P(None, "lon", "lat"),
    )
    return jax.shard_map(
        body,
        mesh=mesh,
        in_specs=placed,
        out_specs=(P(None, None, "lon", "lat"), P()),
        check_vma=False,
    )
```

profile of v0, /device:TPU:0, one launch (start us, length us, event | category | flops | bytes accessed | tf_op | source)
XLA Modules:
  0.0 113.4 jit_solution(7875513095508501059)
XLA Ops:
  0.6 0.0 copy-start
  0.6 1.1 pad_maximum_fusion.5
  1.7 0.5 collective-permute-start
  2.2 4.1 %collective-permute-start.1 = (f32[13,4,8,128]{3,2,1,0:T(8,128)S(1)}, f32[13,4,8,128]{3,2,1,0:T(8,128)S(1)}, u32[]{:S(2)}, u32[]{:S(2)}) collective-permute-start(f32[13,4,8,128]{3,2,1,0:T(8,128)S(1)} %get-tuple-element.30), channel_id=1, source_target_pairs={{1,0},{2,1},{3,2},{4,3},{5,4},{6,5},{7,6},{0,7},{9,8},{10,9},{11,1... | collective-permute-start | bytes 638984 | tf_op jit(solution)/shard_map/ppermute | solution.py:22
  6.4 3.5 %collective-permute-done = f32[13,4,8,128]{3,2,1,0:T(8,128)S(1)} collective-permute-done((f32[13,4,8,128]{3,2,1,0:T(8,128)S(1)}, f32[13,4,8,128]{3,2,1,0:T(8,128)S(1)}, u32[]{:S(2)}, u32[]{:S(2)}) %collective-permute-start) | collective-permute-done | bytes 213024 | tf_op jit(solution)/shard_map/ppermute | solution.py:20
  9.9 0.0 copy-start.2
  9.9 0.0 collective-permute-done.1
  9.9 0.7 copy-done.2
  10.6 0.0 copy-start.3
  10.6 0.7 copy-done.3
  11.3 0.0 copy-done
  11.3 1.3 %pad_maximum_fusion.1 = f32[13,4,80,128]{3,2,1,0:T(8,128)S(1)} fusion(f32[13,4,8,128]{3,2,1,0:T(8,128)S(1)} %collective-permute-done.1, f32[8,4,64,128]{3,2,1,0:T(8,128)S(1)} %copy-done, f32[1,4,64,128]{3,2,1,0:T(8,128)} %bitcast.59, f32[2,4,64,128]{3,2,1,0:T(8,128)} %param.6, f32[2,4,64,128]{3,2,1,0:T(8,128)} %param.5, ...), kind=kLoop, calls=%fused_computation.73 | loop fusion | flops 2662400 | bytes 4259840 | tf_op jit(solution)/shard_map/concatenate | solution.py:18
  12.6 2.1 %fusion.91 = (f32[13,4,80,8]{3,2,1,0:T(8,128)}, f32[13,4,80,8]{3,2,1,0:T(8,128)S(1)}) fusion(f32[13,4,80,128]{3,2,1,0:T(8,128)S(1)} %pad_maximum_fusion.1), kind=kLoop, calls=%fused_computation.204 | loop fusion | bytes 532480 | tf_op jit(solution)/shard_map/slice | solution.py:17
  14.7 2.2 %copy.36 = f32[13,4,80,8]{2,3,1,0:T(8,128)S(1)} copy(f32[13,4,80,8]{3,2,1,0:T(8,128)} %get-tuple-element.27) | data formatting | bytes 266240 | tf_op jit(solution)/shard_map/slice | solution.py:17
  16.8 4.6 %collective-permute-start.2 = (f32[13,4,80,8]{2,3,1,0:T(8,128)S(1)}, f32[13,4,80,8]{2,3,1,0:T(8,128)}, u32[]{:S(2)}, u32[]{:S(2)}) collective-permute-start(f32[13,4,80,8]{2,3,1,0:T(8,128)S(1)} %copy.36), channel_id=1, source_target_pairs={{0,8},{8,16},{16,24},{1,9},{9,17},{17,25},{2,10},{10,18},{18,26},{... | collective-permute-start | bytes 399368 | tf_op jit(solution)/shard_map/ppermute | solution.py:20
  21.5 1.3 %copy.37 = f32[13,4,80,8]{2,3,1,0:T(8,128)} copy(f32[13,4,80,8]{3,2,1,0:T(8,128)S(1)} %get-tuple-element.28) | data formatting | bytes 266240 | tf_op jit(solution)/shard_map/slice | solution.py:16
  22.7 0.0 copy-start.1
  22.7 1.4 %collective-permute-start.3 = (f32[13,4,80,8]{2,3,1,0:T(8,128)}, f32[13,4,80,8]{2,3,1,0:T(8,128)}, u32[]{:S(2)}, u32[]{:S(2)}) collective-permute-start(f32[13,4,80,8]{2,3,1,0:T(8,128)} %copy.37), channel_id=1, source_target_pairs={{8,0},{16,8},{24,16},{9,1},{17,9},{25,17},{10,2},{18,10},{26,18},{... | collective-permute-start | bytes 399368 | tf_op jit(solution)/shard_map/ppermute | solution.py:22
  24.2 1.9 %collective-permute-done.2 = f32[13,4,80,8]{2,3,1,0:T(8,128)} collective-permute-done((f32[13,4,80,8]{2,3,1,0:T(8,128)S(1)}, f32[13,4,80,8]{2,3,1,0:T(8,128)}, u32[]{:S(2)}, u32[]{:S(2)}) %collective-permute-start.2) | collective-permute-done | bytes 133152 | tf_op jit(solution)/shard_map/ppermute | solution.py:20
  26.1 1.6 %copy.38 = f32[13,4,80,8]{3,2,1,0:T(8,128)S(1)} copy(f32[13,4,80,8]{2,3,1,0:T(8,128)} %collective-permute-done.2) | data formatting | bytes 266240 | tf_op jit(solution)/shard_map/ppermute | solution.py:20
  27.7 5.5 %collective-permute-done.3 = f32[13,4,80,8]{2,3,1,0:T(8,128)} collective-permute-done((f32[13,4,80,8]{2,3,1,0:T(8,128)}, f32[13,4,80,8]{2,3,1,0:T(8,128)}, u32[]{:S(2)}, u32[]{:S(2)}) %collective-permute-start.3) | collective-permute-done | bytes 133152 | tf_op jit(solution)/shard_map/ppermute | solution.py:22
  33.2 2.9 %copy.39 = f32[13,4,80,8]{3,2,1,0:T(8,128)} copy(f32[13,4,80,8]{2,3,1,0:T(8,128)} %collective-permute-done.3) | data formatting | bytes 266240 | tf_op jit(solution)/shard_map/ppermute | solution.py:22
  36.1 0.0 copy-done.1
  36.1 4.9 %pad_maximum_fusion = f32[13,4,80,144]{3,2,1,0:T(8,128)S(1)} fusion(f32[13,4,80,8]{3,2,1,0:T(8,128)} %copy.39, f32[13,4,8,128]{3,2,1,0:T(8,128)} %copy-done.3, f32[8,4,64,128]{3,2,1,0:T(8,128)S(1)} %copy-done, f32[1,4,64,128]{3,2,1,0:T(8,128)} %bitcast.60, f32[2,4,64,128]{3,2,1,0:T(8,128)S(1)} %copy-done.1, f32[2,4,64,128]{3,2,1,0:T(8,128)} %param.5, ...), kind=kLoop, calls=%fused_computation.1 | loop fusion | flops 4193280 | bytes 4792320 | tf_op jit(solution)/shard_map/concatenate | solution.py:18
  41.0 0.1 slice_bitcast_fusion
  41.1 0.4 fusion.59
  41.5 0.4 fusion.55
  41.9 0.4 fusion.49
  42.4 0.4 fusion.87
  42.8 0.4 fusion.81
  43.1 0.4 fusion.75
  43.5 0.4 fusion.71
  43.9 0.1 slice.518
  44.1 0.2 slice_subtract_fusion.4
  44.3 0.2 slice_subtract_fusion.2
  44.6 0.2 slice_subtract_fusion
  44.8 0.2 slice_subtract_fusion.12
  45.1 0.3 slice_subtract_fusion.10
  45.4 0.3 slice_subtract_fusion.8
  45.7 0.3 slice_subtract_fusion.6
  46.0 0.2 slice_subtract_fusion.14
  46.2 2.8 %fusion.11 = f32[8,4,78,142]{3,2,1,0:T(8,128)S(1)} fusion(f32[13,4,80,144]{3,2,1,0:T(8,128)S(1)} %pad_maximum_fusion, f32[142]{0:T(256)S(1)} %and_convert_fusion.7, f32[4,78,142]{2,1,0:T(8,128)S(1)} %get-tuple-element.46, f32[4,78,142]{2,1,0:T(8,128)S(1)} %get-tuple-element.45, f32[4,78,142]{2,1,0:T(8,128)S(1)} %get-tuple-element.65, ...), kind=kLoop, calls=%fused_computation.24 | loop fusion | flops 3544320 | bytes 9215800 | tf_op jit(solution)/shard_map/mul | solution.py:95
  49.0 2.8 %fusion.6 = f32[8,4,76,140]{3,2,1,0:T(8,128)S(1)} fusion(f32[8,4,78,142]{3,2,1,0:T(8,128)S(1)} %fusion.11, f32[140]{0:T(256)S(1)} %and_convert_fusion.6, f32[4,76,140]{2,1,0:T(8,128)S(1)} %get-tuple-element.42, f32[4,76,140]{2,1,0:T(8,128)S(1)} %get-tuple-element.41, f32[4,76,140]{2,1,0:T(8,128)S(1)} %get-tuple-element.67, ...), kind=kLoop, calls=%fused_computation.14 | loop fusion | flops 3404800 | bytes 8853040 | tf_op jit(solution)/shard_map/mul | solution.py:95
  51.8 3.0 %fusion.1 = f32[8,4,74,138]{3,2,1,0:T(8,128)S(1)} fusion(f32[8,4,76,140]{3,2,1,0:T(8,128)S(1)} %fusion.6, f32[138]{0:T(256)S(1)} %and_convert_fusion.5, f32[4,74,138]{2,1,0:T(8,128)S(1)} %get-tuple-element.38, f32[4,74,138]{2,1,0:T(8,128)S(1)} %get-tuple-element.37, f32[4,74,138]{2,1,0:T(8,128)S(1)} %get-tuple-element.69, f32[4,74,138]{2,1,0:T(8,128)S(1)} %get-tuple-element.70), kind=kLoop, calls=%fused_computation.4 | loop fusion | flops 3267840 | bytes 8496936 | tf_op jit(solution)/shard_map/mul | solution.py:95
  54.8 2.5 %fusion.32 = f32[8,4,72,136]{3,2,1,0:T(8,128)S(1)} fusion(f32[8,4,74,138]{3,2,1,0:T(8,128)S(1)} %fusion.1, f32[4,72,136]{2,1,0:T(8,128)S(1)} %slice.518, f32[136]{0:T(256)S(1)} %and_convert_fusion.4, f32[4,72,136]{2,1,0:T(8,128)S(1)} %get-tuple-element.34, f32[4,72,136]{2,1,0:T(8,128)S(1)} %get-tuple-element.33, f32[4,72,136]{2,1,0:T(8,128)S(1)} %get-tuple-element.71, ...), kind=kLoop, calls=%fused_computation.65 | loop fusion | flops 3446784 | bytes 8304160 | tf_op jit(solution)/shard_map/mul | solution.py:98
  57.3 2.5 %fusion.26 = f32[8,4,70,134]{3,2,1,0:T(8,128)S(1)} fusion(f32[8,4,72,136]{3,2,1,0:T(8,128)S(1)} %fusion.32, f32[134]{0:T(256)S(1)} %and_convert_fusion.3, f32[4,70,134]{2,1,0:T(8,128)S(1)} %get-tuple-element.62, f32[4,70,134]{2,1,0:T(8,128)S(1)} %get-tuple-element.61, f32[4,70,134]{2,1,0:T(8,128)S(1)} %get-tuple-element.73, ...), kind=kLoop, calls=%fused_computation.54 | loop fusion | flops 3001600 | bytes 7804696 | tf_op jit(solution)/shard_map/mul | solution.py:107
  59.8 2.5 %fusion.21 = f32[8,4,68,132]{3,2,1,0:T(8,128)S(1)} fusion(f32[8,4,70,134]{3,2,1,0:T(8,128)S(1)} %fusion.26, f32[132]{0:T(256)S(1)} %and_convert_fusion.2, f32[4,68,132]{2,1,0:T(8,128)S(1)} %get-tuple-element.58, f32[4,68,132]{2,1,0:T(8,128)S(1)} %get-tuple-element.57, f32[4,68,132]{2,1,0:T(8,128)S(1)} %get-tuple-element.75, ...), kind=kLoop, calls=%fused_computation.44 | loop fusion | flops 2872320 | bytes 7468560 | tf_op jit(solution)/shard_map/mul | solution.py:107
  62.4 2.8 %fusion.16 = f32[8,4,66,130]{3,2,1,0:T(8,128)S(1)} fusion(f32[8,4,68,132]{3,2,1,0:T(8,128)S(1)} %fusion.21, f32[130]{0:T(256)S(1)} %and_convert_fusion.1, f32[4,66,130]{2,1,0:T(8,128)S(1)} %get-tuple-element.54, f32[4,66,130]{2,1,0:T(8,128)S(1)} %get-tuple-element.53, f32[4,66,130]{2,1,0:T(8,128)S(1)} %get-tuple-element.77, ...), kind=kLoop, calls=%fused_computation.34 | loop fusion | flops 2745600 | bytes 7139080 | tf_op jit(solution)/shard_map/mul | solution.py:107
  65.1 1.2 %fusion.39 = f32[8,4,64,128]{3,2,1,0:T(8,128)S(1)} fusion(f32[8,4,66,130]{3,2,1,0:T(8,128)S(1)} %fusion.16, f32[128]{0:T(128)S(1)} %and_convert_fusion, f32[4,64,128]{2,1,0:T(8,128)S(1)} %get-tuple-element.50, f32[4,64,128]{2,1,0:T(8,128)S(1)} %get-tuple-element.49, f32[4,64,128]{2,1,0:T(8,128)S(1)} %get-tuple-element.79, f32[4,64,128]{2,1,0:T(8,128)S(1)} %get-tuple-element.80), kind=kLoop, calls=%fused_computation.79 | loop fusion | flops 2621440 | bytes 6816256 | tf_op jit(solution)/shard_map/mul | solution.py:107
  66.3 2.5 %convolution_bitcast_fusion = f32[8,8]{0,1:T(8,128)S(1)} fusion(f32[8,4,64,128]{3,2,1,0:T(8,128)S(1)} %fusion.39), kind=kOutput, calls=%fused_computation.74 | convolution fusion | flops 25165824 | bytes 1048832 | tf_op jit(solution)/shard_map/pc,qc->pq/dot_general | solution.py:110
  68.8 38.4 %psum.7 = f32[8,8]{0,1:T(8,128)S(1)} all-reduce(f32[8,8]{0,1:T(8,128)S(1)} %convolution_bitcast_fusion), channel_id=1, replica_groups=mesh['lat'=4,'lon'=8] {'lat','lon'}, use_global_device_ids=true, to_apply=%region_0.0 | all-reduce | flops 64 | bytes 512 | tf_op jit(solution)/shard_map/psum | solution.py:110
  107.2 0.1 copy.43
  107.2 0.7 cholesky.17
  108.0 0.6 compare_reduce_fusion
  108.6 0.6 multiply_bitcast_fusion
  109.3 0.6 custom-call.6
  109.9 0.2 fusion.88
  110.1 1.5 %convolution_multiply_fusion = f32[8,32768]{1,0:T(8,128)S(1)} fusion(f32[8,8]{1,0:T(8,128)S(1)} %fusion.88, f32[1,8,256,128]{3,2,1,0:T(8,128)S(1)} %bitcast.56), kind=kOutput, calls=%fused_computation | convolution fusion | flops 25427968 | bytes 2097408 | tf_op jit(solution)/shard_map/dot_general | solution.py:112
  111.6 1.2 %copy.45 = f32[8,4,64,128]{3,2,1,0:T(8,128)} copy(f32[8,4,64,128]{3,0,2,1:T(8,128)S(1)} %bitcast.57) | data formatting | bytes 2097152
  112.8 0.7 copy.46
  (10 shorter events, 0.1 us)
Async XLA Ops:
  0.6 10.7 %copy-start = (f32[8,4,64,128]{3,2,1,0:T(8,128)S(1)}, f32[8,4,64,128]{3,2,1,0:T(8,128)}, u32[]{:S(2)}) copy-start(f32[8,4,64,128]{3,2,1,0:T(8,128)} %param.4) | copy-start | bytes 3145732
  1.7 8.2 %collective-permute-start = (f32[13,4,8,128]{3,2,1,0:T(8,128)S(1)}, f32[13,4,8,128]{3,2,1,0:T(8,128)S(1)}, u32[]{:S(2)}, u32[]{:S(2)}) collective-permute-start(f32[13,4,8,128]{3,2,1,0:T(8,128)S(1)} %get-tuple-element.29), channel_id=1, source_target_pairs={{0,1},{1,2},{2,3},{3,4},{4,5},{5,6},{6,7},{7,0},{8,9},{9,10},{10,1... | collective-permute-start | bytes 638984 | tf_op jit(solution)/shard_map/ppermute | solution.py:20
  2.2 7.7 %collective-permute-start.1 = (f32[13,4,8,128]{3,2,1,0:T(8,128)S(1)}, f32[13,4,8,128]{3,2,1,0:T(8,128)S(1)}, u32[]{:S(2)}, u32[]{:S(2)}) collective-permute-start(f32[13,4,8,128]{3,2,1,0:T(8,128)S(1)} %get-tuple-element.30), channel_id=1, source_target_pairs={{1,0},{2,1},{3,2},{4,3},{5,4},{6,5},{7,6},{0,7},{9,8},{10,9},{11,1... | collective-permute-start | bytes 638984 | tf_op jit(solution)/shard_map/ppermute | solution.py:22
  9.9 0.7 copy-start.2
  10.6 0.7 copy-start.3
  16.8 9.3 %collective-permute-start.2 = (f32[13,4,80,8]{2,3,1,0:T(8,128)S(1)}, f32[13,4,80,8]{2,3,1,0:T(8,128)}, u32[]{:S(2)}, u32[]{:S(2)}) collective-permute-start(f32[13,4,80,8]{2,3,1,0:T(8,128)S(1)} %copy.36), channel_id=1, source_target_pairs={{0,8},{8,16},{16,24},{1,9},{9,17},{17,25},{2,10},{10,18},{18,26},{... | collective-permute-start | bytes 399368 | tf_op jit(solution)/shard_map/ppermute | solution.py:20
  22.7 13.4 %copy-start.1 = (f32[2,4,64,128]{3,2,1,0:T(8,128)S(1)}, f32[2,4,64,128]{3,2,1,0:T(8,128)}, u32[]{:S(2)}) copy-start(f32[2,4,64,128]{3,2,1,0:T(8,128)} %param.6) | copy-start | bytes 786436
  22.7 10.5 %collective-permute-start.3 = (f32[13,4,80,8]{2,3,1,0:T(8,128)}, f32[13,4,80,8]{2,3,1,0:T(8,128)}, u32[]{:S(2)}, u32[]{:S(2)}) collective-permute-start(f32[13,4,80,8]{2,3,1,0:T(8,128)} %copy.37), channel_id=1, source_target_pairs={{8,0},{16,8},{24,16},{9,1},{17,9},{25,17},{10,2},{18,10},{26,18},{... | collective-permute-start | bytes 399368 | tf_op jit(solution)/shard_map/ppermute | solution.py:22
where the time goes:
time: 114 us; the launch traced here: 113 us
  blocking collectives  38.4 us (34%)
  other arithmetic  35 us (31%)
  local copies, waits for them, and re-layouts  13.4 us (12%)
  waiting for transfers between devices  11 us (10%)
  starting transfers between devices  10.7 us (9%)
  matrix products  4.18 us (4%)
    psum x1, blocking collectives, body(): lax.psum(jnp.einsum('pc,qc->pq', flat, flat, precision=high), ('lat', 'lo...  38.4 us
    mul x7, other arithmetic, body(): field = field * lat_mask(radius)  17.6 us
    concatenate x2, other arithmetic, padded(): jnp.concatenate([lax.ppermute(tail, axis, [(i, (i + 1) % count) for i in...  6.1 us
    ppermute x2, waiting for transfers between devices, padded(): lax.ppermute(head, axis, [((i + 1) % count, i) for i in range(ends)])  5.52 us
    ppermute x2, starting transfers between devices, padded(): lax.ppermute(head, axis, [((i + 1) % count, i) for i in range(ends)])  5.51 us
    ppermute x2, waiting for transfers between devices, padded(): lax.ppermute(tail, axis, [(i, (i + 1) % count) for i in range(ends)])  5.45 us
    ppermute x2, starting transfers between devices, padded(): lax.ppermute(tail, axis, [(i, (i + 1) % count) for i in range(ends)])  5.14 us
    slice x2, local copies, waits for them, and re-layouts, padded(): lax.slice_in_dim(cells, cells.shape[dim] - width, cells.shape[dim], axis=...  4.24 us
  transfers between devices with their start and end apart: 4, of which 3 were waited for; matrix products, arithmetic and copies ran while one was open for 3% of the time, Pallas kernels for 0%

commit v1 on v0

v1 whole, which is shorter than its diff:
```python
import functools
import jax
import jax.numpy as jnp
from jax import lax
from jax.experimental import pallas as pl
from jax.experimental.pallas import tpu as pltpu
from jax.sharding import PartitionSpec as P

STEPS = 4
DIFFUSE = 0.24
CENTRE = 1.0 - 4.0 * DIFFUSE
MESH = pl.DeviceIdType.MESH

HALO = 2 * STEPS
OWN = 2 * HALO
WINDOW = 32


def window_shift(side, level, width):
    if side == 0:
        return (WINDOW * level + HALO) % width
    return (WINDOW * level - (width - WINDOW + HALO)) % width


def transport_kernel(
    n_lat, n_lon, probes, wind, tend, weight, z_out, tile_out,
    field, other, masks, z_buf, send_pack, recv_pack, sums, part,
    load_sem, z_sem, lon_send, lon_recv, lat_send, lat_recv,
    sum_send, sum_recv, part_send, part_recv,
):
    count, levels, rows, width = probes.shape
    entities = count + 5
    lat = lax.axis_index("lat")
    lon = lax.axis_index("lon")
    up_lon, down_lon = lax.rem(lon + 1, n_lon), lax.rem(lon + n_lon - 1, n_lon)
    up_lat, down_lat = lax.rem(lat + 1, n_lat), lax.rem(lat + n_lat - 1, n_lat)
    lane = lax.broadcasted_iota(jnp.int32, (8, width), 1)
    row = lax.broadcasted_iota(jnp.int32, (8, width), 0)
    in_window = lane % WINDOW

    barrier = pltpu.get_barrier_semaphore()

    def greet(to_lat, to_lon):
        pl.semaphore_signal(barrier, inc=1, device_id=(to_lat, to_lon), device_id_type=MESH)

    for k in range(1, n_lon):
        greet(lat, lax.rem(lon + k, n_lon))
    for k in range(1, n_lat):
        greet(lax.rem(lat + k, n_lat), lon)
    for to_lat in (up_lat, down_lat):
        for to_lon in (up_lon, down_lon):
            greet(to_lat, to_lon)

    placed = ((probes, 0, count), (wind, count, 2), (tend, count + 2, 2), (weight, count + 4, 1))
    loads = [
        pltpu.make_async_copy(
            source,
            field.at[pl.ds(first, size), pl.ds(0, levels), pl.ds(OWN, rows), :],
            load_sem.at[k],
        )
        for k, (source, first, size) in enumerate(placed)
    ]
    for load in loads:
        load.start()

    zero = jnp.zeros((8, width), jnp.float32)
    for buffer, size in ((field, entities), (other, count)):
        for start in (0, OWN + rows + HALO):
            buffer[:, :, pl.ds(start, 8), :] = jnp.zeros((size, levels + 2, 8, width), jnp.float32)
    total = width * n_lat
    for level in range(levels):
        masks[level] = jnp.ones((8, width), jnp.float32)
    for side, first in ((0, -HALO), (1, width - WINDOW + HALO)):
        column = lat * width + first + in_window
        masks[levels + side] = jnp.where((column >= 0) & (column < total), 1.0, 0.0)

    pl.semaphore_wait(barrier, n_lon + n_lat + 2)

    lon_copies = []
    for d, (to_lon, src_row, dst_row) in enumerate(
        ((up_lon, rows - HALO, HALO), (down_lon, 0, OWN + rows))
    ):
        for k, (source, first, size) in enumerate(placed):
            copy = pltpu.make_async_remote_copy(
                src_ref=source.at[:, :, pl.ds(src_row, HALO), :],
                dst_ref=field.at[pl.ds(first, size), pl.ds(0, levels), pl.ds(dst_row, HALO), :],
                send_sem=lon_send.at[d, k],
                recv_sem=lon_recv.at[d, k],
                device_id=(lat, to_lon),
                device_id_type=MESH,
            )
            copy.start()
            lon_copies.append(copy)

    def own_window(entity, side, start):
        made = None
        for level in range(levels):
            piece = pltpu.roll(
                field[entity, level, pl.ds(start, 8), :], window_shift(side, level, width), 1
            )
            made = piece if made is None else jnp.where(lane >= WINDOW * level, piece, made)
        return made

    for load in loads:
        load.wait()

    def pack(group, carry):
        start = pl.multiple_of(OWN + 8 * group, 8)
        to = pl.multiple_of(8 * group, 8)
        for side in range(2):
            packed = [zero] * ((entities + 3) // 4)
            for entity in range(entities):
                made = own_window(entity, side, start)
                field[entity, levels + side, pl.ds(start, 8), :] = made
                slot = entity % 4
                moved = pltpu.roll(made, (8 * slot - (8 if side == 0 else 16)) % width, 1)
                packed[entity // 4] = jnp.where(
                    in_window // 8 == slot, moved, packed[entity // 4]
                )
            for k, value in enumerate(packed):
                send_pack[side, k, pl.ds(to, 8), :] = value
        return carry

    lax.fori_loop(0, rows // 8, pack, 0)

    has = (lat > 0, lat < n_lat - 1)
    lat_copies = ([], [])
    for side, to_lat in ((0, down_lat), (1, up_lat)):
        for k, (to_lon, src_row, size, dst_row) in enumerate(
            (
                (lon, 0, rows, HALO),
                (up_lon, rows - HALO, HALO, 0),
                (down_lon, 0, HALO, HALO + rows),
            )
        ):
            lat_copies[side].append(
                pltpu.make_async_remote_copy(
                    src_ref=send_pack.at[side, :, pl.ds(src_row, size), :],
                    dst_ref=recv_pack.at[1 - side, :, pl.ds(dst_row, size), :],
                    send_sem=lat_send.at[side, k],
                    recv_sem=lat_recv.at[side, k],
                    device_id=(to_lat, to_lon),
                    device_id_type=MESH,
                )
            )

    for side in range(2):
        @pl.when(has[side])
        def _():
            for copy in lat_copies[side]:
                copy.start()

    for copy in lon_copies:
        copy.wait_recv()

    for start in (HALO, OWN + rows):
        for entity in range(entities):
            for side in range(2):
                field[entity, levels + side, pl.ds(start, 8), :] = own_window(entity, side, start)

    for side in range(2):
        @pl.when(has[side])
        def _():
            for copy in lat_copies[1 - side]:
                copy.wait_recv()

        @pl.when(jnp.logical_not(has[side]))
        def _():
            recv_pack[side] = jnp.zeros(recv_pack.shape[1:], jnp.float32)

    def unpack(group, carry):
        start = pl.multiple_of(HALO + 8 * group, 8)
        at = pl.multiple_of(8 * group, 8)
        for side in range(2):
            here = in_window < 8 if side == 0 else in_window >= 24
            for entity in range(entities):
                slot = entity % 4
                got = recv_pack[side, entity // 4, pl.ds(at, 8), :]
                moved = pltpu.roll(got, ((0 if side == 0 else 24) - 8 * slot) % width, 1)
                held = field[entity, levels + side, pl.ds(start, 8), :]
                field[entity, levels + side, pl.ds(start, 8), :] = jnp.where(here, moved, held)
        return carry

    groups = rows // 8 + 2
    lax.fori_loop(0, groups, unpack, 0)

    def rate(which, step, level, start):
        now = field[count + which, level, pl.ds(start, 8), :]
        if step:
            now = now + step * field[count + 2 + which, level, pl.ds(start, 8), :]
        return 0.5 * now

    def run_step(source, target, step, adjoint):
        def body(index, carry):
            level = index // groups
            start = pl.multiple_of(HALO + 8 * (index % groups), 8)
            mask = masks[level]
            if adjoint:
                north = rate(1, step, level, start)
                before = mask * (DIFFUSE - rate(0, step, level, start - 1))
                after = mask * (DIFFUSE + rate(0, step, level, start + 1))
                left = mask * pltpu.roll(DIFFUSE - north, 1, 1)
                right = mask * pltpu.roll(DIFFUSE + north, width - 1, 1)
            else:
                if step == STEPS - 1:
                    mask = mask * field[count + 4, level, pl.ds(start, 8), :]
                east = rate(0, step, level, start)
                north = rate(1, step, level, start)
                after = mask * (DIFFUSE - east)
                before = mask * (DIFFUSE + east)
                right = mask * (DIFFUSE - north)
                left = mask * (DIFFUSE + north)
            centre = CENTRE * mask
            for probe in range(count):
                middle = source[probe, level, pl.ds(start, 8), :]
                target[probe, level, pl.ds(start, 8), :] = (
                    (centre * middle + after * source[probe, level, pl.ds(start + 1, 8), :])
                    + (before * source[probe, level, pl.ds(start - 1, 8), :]
                       + right * pltpu.roll(middle, width - 1, 1))
                    + left * pltpu.roll(middle, 1, 1)
                )
            return carry

        lax.fori_loop(0, (levels + 2) * groups, body, 0)

    source, target = field, other
    for step in range(STEPS):
        run_step(source, target, step, False)
        source, target = target, source
    for step in reversed(range(STEPS)):
        run_step(source, target, step, True)
        source, target = target, source

    pairs = [(p, q) for p in range(count) for q in range(p, count)]

    accs = [zero] * len(pairs)
    for level in range(levels):
        def gather(group, accs):
            start = pl.multiple_of(OWN + 8 * group, 8)
            to = pl.multiple_of(8 * group, 8)
            values = []
            for probe in range(count):
                first = pltpu.roll(
                    source[probe, levels, pl.ds(start, 8), :],
                    (width - window_shift(0, level, width)) % width, 1,
                )
                last = pltpu.roll(
                    source[probe, levels + 1, pl.ds(start, 8), :],
                    (width - window_shift(1, level, width)) % width, 1,
                )
                value = source[probe, level, pl.ds(start, 8), :]
                value = jnp.where(lane < HALO, first, value)
                value = jnp.where(lane >= width - HALO, last, value)
                z_buf[probe, level, pl.ds(to, 8), :] = value
                values.append(value)
            return tuple(a + values[p] * values[q] for a, (p, q) in zip(accs, pairs))

        accs = lax.fori_loop(0, rows // 8, gather, tuple(accs))

    z_copy = pltpu.make_async_copy(z_buf, z_out, z_sem)
    z_copy.start()

    reduced = {
        pair: jnp.broadcast_to(jnp.sum(acc, axis=0, keepdims=True), (8, width))
        for pair, acc in zip(pairs, accs)
    }
    gram = zero
    for q in range(count):
        column = zero
        for p in range(count):
            column = jnp.where(row == p, reduced[(min(p, q), max(p, q))], column)
        gram = jnp.where(lane == q, jnp.sum(column, axis=1, keepdims=True), gram)

    def all_sum(value, slots, size, me, peer, send, recv):
        slots[me] = value
        copies = []
        for k in range(1, size):
            copy = pltpu.make_async_remote_copy(
                src_ref=slots.at[me],
                dst_ref=slots.at[me],
                send_sem=send.at[k],
                recv_sem=recv.at[k],
                device_id=peer(lax.rem(me + k, size)),
                device_id_type=MESH,
            )
            copy.start()
            copies.append(copy)
        for k, copy in enumerate(copies):
            came = lax.rem(me + size - (k + 1), size)
            pltpu.make_async_remote_copy(
                src_ref=slots.at[came],
                dst_ref=slots.at[came],
                send_sem=send.at[k + 1],
                recv_sem=recv.at[k + 1],
                device_id=peer(lax.rem(me + k + 1, size)),
                device_id_type=MESH,
            ).wait_recv()
        out = slots[0]
        for k in range(1, size):
            out = out + slots[k]
        return out, copies

    gram, first_copies = all_sum(gram, sums, n_lon, lon, lambda i: (lat, i), sum_send, sum_recv)
    gram, last_copies = all_sum(gram, part, n_lat, lat, lambda i: (i, lon), part_send, part_recv)

    work = jnp.where(lane == row + count, 1.0, jnp.where(lane < count, gram, 0.0))
    result = zero
    for k in range(count):
        pivot = work[k : k + 1, :]
        diagonal = pivot[:, k : k + 1]
        pivot = pivot * (1.0 / jnp.sqrt(diagonal))
        result = jnp.where((row == k) & (lane >= k), pivot, result)
        work = work - jnp.where(row > k, (work[:, k : k + 1] * (1.0 / diagonal)), 0.0) * work[k : k + 1, :]
    tile_out[...] = result

    for copy in first_copies + last_copies:
        copy.wait_send()
    for copy in lon_copies:
        copy.wait_send()
    for side in range(2):
        @pl.when(has[side])
        def _():
            for copy in lat_copies[side]:
                copy.wait_send()
    z_copy.wait()


def apply_kernel(scale, inverse, tile, z, basis, factor):
    count, _, rows, width = z.shape
    coefficients = [
        [inverse[p, count + q] * scale for q in range(p + 1)] for p in range(count)
    ]
    for start in range(0, rows, 8):
        values = [z[q, 0, pl.ds(start, 8), :] for q in range(count)]
        for p in range(count):
            total = coefficients[p][0] * values[0]
            for q in range(1, p + 1):
                total = total + coefficients[p][q] * values[q]
            basis[p, 0, pl.ds(start, 8), :] = total

    @pl.when(pl.program_id(0) == 0)
    def _():
        factor[...] = tile[:, :count] * (1.0 / scale)


def body(probes, wind, wind_tend, obs_weight, *, n_lat, n_lon):
    count, levels, rows, width = probes.shape
    entities = count + 5
    packs = (entities + 3) // 4
    tall = rows + 4 * HALO
    f32 = jnp.float32
    z, tile = pl.pallas_call(
        functools.partial(transport_kernel, n_lat, n_lon),
        out_shape=(
            jax.ShapeDtypeStruct(probes.shape, f32),
            jax.ShapeDtypeStruct((8, width), f32),
        ),
        in_specs=[pl.BlockSpec(memory_space=pl.ANY)] * 4,
        out_specs=(
            pl.BlockSpec(memory_space=pl.ANY),
            pl.BlockSpec(memory_space=pltpu.VMEM),
        ),
        scratch_shapes=[
            pltpu.VMEM((entities, levels + 2, tall, width), f32),
            pltpu.VMEM((count, levels + 2, tall, width), f32),
            pltpu.VMEM((levels + 2, 8, width), f32),
            pltpu.VMEM(probes.shape, f32),
            pltpu.VMEM((2, packs, rows, width), f32),
            pltpu.VMEM((2, packs, rows + 2 * HALO, width), f32),
            pltpu.VMEM((n_lon, 8, width), f32),
            pltpu.VMEM((n_lat, 8, width), f32),
            pltpu.SemaphoreType.DMA((4,)),
            pltpu.SemaphoreType.DMA,
            pltpu.SemaphoreType.DMA((2, 4)),
            pltpu.SemaphoreType.DMA((2, 4)),
            pltpu.SemaphoreType.DMA((2, 3)),
            pltpu.SemaphoreType.DMA((2, 3)),
            pltpu.SemaphoreType.DMA((n_lon,)),
            pltpu.SemaphoreType.DMA((n_lon,)),
            pltpu.SemaphoreType.DMA((n_lat,)),
            pltpu.SemaphoreType.DMA((n_lat,)),
        ],
        compiler_params=pltpu.CompilerParams(
            collective_id=0, has_side_effects=True, vmem_limit_bytes=32 * 2**20
        ),
        name="transport",
    )(probes, wind, wind_tend, obs_weight[None])

    cells = levels * rows * width * n_lat * n_lon
    block = pl.BlockSpec((count, 1, rows, width), lambda level: (0, level, 0, 0))
    basis, factor = pl.pallas_call(
        functools.partial(apply_kernel, float(cells) ** 0.5),
        grid=(levels,),
        out_shape=(
            jax.ShapeDtypeStruct(probes.shape, f32),
            jax.ShapeDtypeStruct((count, count), f32),
        ),
        in_specs=[
            pl.BlockSpec(memory_space=pltpu.SMEM),
            pl.BlockSpec((8, width), lambda level: (0, 0)),
            block,
        ],
        out_specs=(block, pl.BlockSpec((count, count), lambda level: (0, 0))),
        compiler_params=pltpu.CompilerParams(vmem_limit_bytes=16 * 2**20),
        name="orthonormal",
    )(tile, tile, z)
    return basis, factor


def solution(mesh):
    placed = (
        P(None, None, "lon", "lat"),
        P(None, None, "lon", "lat"),
        P(None, None, "lon", "lat"),
        P(None, "lon", "lat"),
    )
    return jax.shard_map(
        functools.partial(body, n_lat=mesh.shape["lat"], n_lon=mesh.shape["lon"]),
        mesh=mesh,
        in_specs=placed,
        out_specs=(P(None, None, "lon", "lat"), P()),
        check_vma=False,
    )
```

time: 114 us -> 84.4 us (0.74)
  Pallas kernels: 0 us -> 79.5 us
  blocking collectives: 38.4 us -> 0 us
  other arithmetic: 35 us -> 0 us
  waiting for transfers between devices: 11 us -> 0 us
  starting transfers between devices: 10.7 us -> 0 us
  local copies, waits for them, and re-layouts: 13.4 us -> 4.02 us
  matrix products: 4.18 us -> 0 us
    pallas_call x0 -> x2, Pallas kernels: none -> 79.5 us  [the longest x1 77.2 us: body(): pl.pallas_call(functools.partial(transport_kernel, n_lat, n_lon), out_sha...]
    psum x1 -> x0, blocking collectives: 38.4 us -> none  [body(): lax.psum(jnp.einsum('pc,qc->pq', flat, flat, precision=high), ('lat', 'lo...]
    mul x15 -> x0, other arithmetic: 22.9 us -> none  [the longest x7 17.6 us: body(): field = field * lat_mask(radius)]
    ppermute x4 -> x0, waiting for transfers between devices: 11 us -> none  [the longest x2 5.52 us: padded(): lax.ppermute(head, axis, [((i + 1) % count, i) for i in range(ends)])]
    ppermute x4 -> x0, starting transfers between devices: 10.7 us -> none  [the longest x2 5.51 us: padded(): lax.ppermute(head, axis, [((i + 1) % count, i) for i in range(ends)])]
    concatenate x2 -> x0, other arithmetic: 6.1 us -> none  [padded(): jnp.concatenate([lax.ppermute(tail, axis, [(i, (i + 1) % count) for i in...]
    slice x4 -> x0, local copies, waits for them, and re-layouts: 5.66 us -> none  [the longest x2 4.24 us: padded(): lax.slice_in_dim(cells, cells.shape[dim] - width, cells.shape[dim], axis=...]
    ppermute x2 -> x0, local copies, waits for them, and re-layouts: 4.46 us -> none  [the longest x1 2.91 us: padded(): lax.ppermute(head, axis, [((i + 1) % count, i) for i in range(ends)])]
  transfers between devices with their start and end apart: 4 -> 0, of which waited for: 3 -> 0; matrix products, arithmetic and copies ran while one was open for 3% -> 0% of each run, Pallas kernels for 0% -> 0%
where the time goes in v1:
time: 84.4 us; the launch traced here: 84.2 us
  Pallas kernels  79.5 us (94%)
  local copies, waits for them, and re-layouts  4.02 us (5%)
    pallas_call x1, Pallas kernels, body(): pl.pallas_call(functools.partial(transport_kernel, n_lat, n_lon), out_sha...  77.2 us
    unnamed x8, local copies, waits for them, and re-layouts  4.02 us
    pallas_call x1, Pallas kernels, body(): pl.pallas_call(functools.partial(apply_kernel, float(cells) ** 0.5), grid...  2.37 us

profile of v1, /device:TPU:0, one launch (start us, length us, event | category | flops | bytes accessed | tf_op | source)
XLA Modules:
  0.0 84.2 jit_solution(2955647404544494988)
XLA Ops:
  0.6 0.0 copy-start
  0.6 1.2 %copy-done = f32[8,4,64,128]{3,2,1,0:T(8,128)S(1)} copy-done((f32[8,4,64,128]{3,2,1,0:T(8,128)S(1)}, f32[8,4,64,128]{3,2,1,0:T(8,128)}, u32[]{:S(2)}) %copy-start) | copy-done | bytes 1048600
  1.9 0.0 copy-start.1
  1.9 0.9 %copy-done.1 = f32[2,4,64,128]{3,2,1,0:T(8,128)S(1)} copy-done((f32[2,4,64,128]{3,2,1,0:T(8,128)S(1)}, f32[2,4,64,128]{3,2,1,0:T(8,128)}, u32[]{:S(2)}) %copy-start.1) | copy-done | bytes 262168
  2.8 0.0 copy-start.2
  2.8 0.9 %copy-done.2 = f32[2,4,64,128]{3,2,1,0:T(8,128)S(1)} copy-done((f32[2,4,64,128]{3,2,1,0:T(8,128)S(1)}, f32[2,4,64,128]{3,2,1,0:T(8,128)}, u32[]{:S(2)}) %copy-start.2) | copy-done | bytes 262168
  3.8 0.0 copy-start.3
  3.8 0.9 %copy-done.3 = f32[4,64,128]{2,1,0:T(8,128)S(1)} copy-done((f32[4,64,128]{2,1,0:T(8,128)S(1)}, f32[4,64,128]{2,1,0:T(8,128)}, u32[]{:S(2)}) %copy-start.3) | copy-done | bytes 131096
  4.7 77.2 %transport.1 = (f32[8,4,64,128]{3,2,1,0:T(8,128)S(1)}, f32[8,128]{1,0:T(8,128)S(1)}) custom-call(f32[8,4,64,128]{3,2,1,0:T(8,128)S(1)} %copy-done, f32[2,4,64,128]{3,2,1,0:T(8,128)S(1)} %copy-done.1, f32[2,4,64,128]{3,2,1,0:T(8,128)S(1)} %copy-done.2, f32[1,4,64,128]{3,2,1,0:T(8,128)S(1)} %bitcast.1), custom_call_target="tpu_custom_call" | custom-call | tf_op jit(solution)/shard_map/transport/pallas_call | solution.py:352
  81.8 2.4 %orthonormal.1 = (f32[8,4,64,128]{3,2,1,0:T(8,128)}, f32[8,8]{1,0:T(8,128)}) custom-call(f32[8,128]{1,0:T(8,128)S(1)} %get-tuple-element.4.inverse.tile, f32[8,128]{1,0:T(8,128)S(1)} %get-tuple-element.4.inverse.tile, f32[8,4,64,128]{3,2,1,0:T(8,128)S(1)} %get-tuple-element.5.z), custom_call_target="tpu_custom_call" | custom-call | tf_op jit(solution)/shard_map/orthonormal/pallas_call | solution.py:391
Async XLA Ops:
  0.6 1.2 %copy-start = (f32[8,4,64,128]{3,2,1,0:T(8,128)S(1)}, f32[8,4,64,128]{3,2,1,0:T(8,128)}, u32[]{:S(2)}) copy-start(f32[8,4,64,128]{3,2,1,0:T(8,128)} %probes.1) | copy-start | bytes 3145732
  1.9 0.9 %copy-start.1 = (f32[2,4,64,128]{3,2,1,0:T(8,128)S(1)}, f32[2,4,64,128]{3,2,1,0:T(8,128)}, u32[]{:S(2)}) copy-start(f32[2,4,64,128]{3,2,1,0:T(8,128)} %wind.1) | copy-start | bytes 786436
  2.8 0.9 %copy-start.2 = (f32[2,4,64,128]{3,2,1,0:T(8,128)S(1)}, f32[2,4,64,128]{3,2,1,0:T(8,128)}, u32[]{:S(2)}) copy-start(f32[2,4,64,128]{3,2,1,0:T(8,128)} %tend.1) | copy-start | bytes 786436
  3.8 0.9 %copy-start.3 = (f32[4,64,128]{2,1,0:T(8,128)S(1)}, f32[4,64,128]{2,1,0:T(8,128)}, u32[]{:S(2)}) copy-start(f32[4,64,128]{2,1,0:T(8,128)} %param.7) | copy-start | bytes 393220

commit v2 on v1

--- a/solution.py
+++ b/solution.py
@@ -182,7 +182,7 @@
         return carry
 
     groups = rows // 8 + 2
-    lax.fori_loop(0, groups, unpack, 0)
+    lax.fori_loop(0, groups, unpack, 0, unroll=2)
 
     def rate(which, step, level, start):
         now = field[count + which, level, pl.ds(start, 8), :]
@@ -190,45 +190,46 @@
             now = now + step * field[count + 2 + which, level, pl.ds(start, 8), :]
         return 0.5 * now
 
-    def run_step(source, target, step, adjoint):
-        def body(index, carry):
-            level = index // groups
-            start = pl.multiple_of(HALO + 8 * (index % groups), 8)
-            mask = masks[level]
-            if adjoint:
-                north = rate(1, step, level, start)
-                before = mask * (DIFFUSE - rate(0, step, level, start - 1))
-                after = mask * (DIFFUSE + rate(0, step, level, start + 1))
-                left = mask * pltpu.roll(DIFFUSE - north, 1, 1)
-                right = mask * pltpu.roll(DIFFUSE + north, width - 1, 1)
-            else:
-                if step == STEPS - 1:
-                    mask = mask * field[count + 4, level, pl.ds(start, 8), :]
-                east = rate(0, step, level, start)
-                north = rate(1, step, level, start)
-                after = mask * (DIFFUSE - east)
-                before = mask * (DIFFUSE + east)
-                right = mask * (DIFFUSE - north)
-                left = mask * (DIFFUSE + north)
-            centre = CENTRE * mask
-            for probe in range(count):
-                middle = source[probe, level, pl.ds(start, 8), :]
-                target[probe, level, pl.ds(start, 8), :] = (
-                    (centre * middle + after * source[probe, level, pl.ds(start + 1, 8), :])
-                    + (before * source[probe, level, pl.ds(start - 1, 8), :]
-                       + right * pltpu.roll(middle, width - 1, 1))
-                    + left * pltpu.roll(middle, 1, 1)
-                )
+    def run_step(source, target, step, adjoint, first, last):
+        def body(level, carry):
+            edge = masks[level]
+            for group in range(first, last):
+                start = HALO + 8 * group
+                mask = edge
+                if adjoint:
+                    north = rate(1, step, level, start)
+                    before = mask * (DIFFUSE - rate(0, step, level, start - 1))
+                    after = mask * (DIFFUSE + rate(0, step, level, start + 1))
+                    left = mask * pltpu.roll(DIFFUSE - north, 1, 1)
+                    right = mask * pltpu.roll(DIFFUSE + north, width - 1, 1)
+                else:
+                    if step == STEPS - 1:
+                        mask = mask * field[count + 4, level, pl.ds(start, 8), :]
+                    east = rate(0, step, level, start)
+                    north = rate(1, step, level, start)
+                    after = mask * (DIFFUSE - east)
+                    before = mask * (DIFFUSE + east)
+                    right = mask * (DIFFUSE - north)
+                    left = mask * (DIFFUSE + north)
+                centre = CENTRE * mask
+                for probe in range(count):
+                    middle = source[probe, level, pl.ds(start, 8), :]
+                    target[probe, level, pl.ds(start, 8), :] = (
+                        (centre * middle + after * source[probe, level, pl.ds(start + 1, 8), :])
+                        + (before * source[probe, level, pl.ds(start - 1, 8), :]
+                           + right * pltpu.roll(middle, width - 1, 1))
+                        + left * pltpu.roll(middle, 1, 1)
+                    )
             return carry
 
-        lax.fori_loop(0, (levels + 2) * groups, body, 0)
+        lax.fori_loop(0, levels + 2, body, 0)
 
     source, target = field, other
     for step in range(STEPS):
-        run_step(source, target, step, False)
+        run_step(source, target, step, False, 0, groups)
         source, target = target, source
     for step in reversed(range(STEPS)):
-        run_step(source, target, step, True)
+        run_step(source, target, step, True, int(step == 0), groups - int(step == 0))
         source, target = target, source
 
     pairs = [(p, q) for p in range(count) for q in range(p, count)]
@@ -255,7 +256,7 @@
                 values.append(value)
             return tuple(a + values[p] * values[q] for a, (p, q) in zip(accs, pairs))
 
-        accs = lax.fori_loop(0, rows // 8, gather, tuple(accs))
+        accs = lax.fori_loop(0, rows // 8, gather, tuple(accs), unroll=4)
 
     z_copy = pltpu.make_async_copy(z_buf, z_out, z_sem)
     z_copy.start()
@@ -355,7 +356,7 @@
             jax.ShapeDtypeStruct(probes.shape, f32),
             jax.ShapeDtypeStruct((8, width), f32),
         ),
-        in_specs=[pl.BlockSpec(memory_space=pl.ANY)] * 4,
+        in_specs=[pl.BlockSpec(memory_space=pltpu.HBM)] * 4,
         out_specs=(
             pl.BlockSpec(memory_space=pl.ANY),
             pl.BlockSpec(memory_space=pltpu.VMEM),
@@ -381,7 +382,7 @@
             pltpu.SemaphoreType.DMA((n_lat,)),
         ],
         compiler_params=pltpu.CompilerParams(
-            collective_id=0, has_side_effects=True, vmem_limit_bytes=32 * 2**20
+            collective_id=0, has_side_effects=True, vmem_limit_bytes=60 * 2**20
         ),
         name="transport",
     )(probes, wind, wind_tend, obs_weight[None])
@@ -401,7 +402,7 @@
             block,
         ],
         out_specs=(block, pl.BlockSpec((count, count), lambda level: (0, 0))),
-        compiler_params=pltpu.CompilerParams(vmem_limit_bytes=16 * 2**20),
+        compiler_params=pltpu.CompilerParams(vmem_limit_bytes=60 * 2**20),
         name="orthonormal",
     )(tile, tile, z)
     return basis, factor

time: 84.4 us -> 42.7 us (0.51)
  Pallas kernels: 79.5 us -> 41.9 us
  local copies, waits for them, and re-layouts: 4.02 us -> 0 us
    pallas_call x1, Pallas kernels: 77.2 us -> 38.4 us  [body(): pl.pallas_call(functools.partial(transport_kernel, n_lat, n_lon), out_sha...]
    unnamed x8 -> x0, local copies, waits for them, and re-layouts: 4.02 us -> none
    pallas_call x1, Pallas kernels: 2.37 us -> 3.54 us  [body(): pl.pallas_call(functools.partial(apply_kernel, float(cells) ** 0.5), grid...]
where the time goes in v2:
time: 42.7 us; the launch traced here: 42.5 us
  Pallas kernels  41.9 us (98%)
  between operations  0.64 us (1%)
    pallas_call x1, Pallas kernels, body(): pl.pallas_call(functools.partial(transport_kernel, n_lat, n_lon), out_sha...  38.4 us
    pallas_call x1, Pallas kernels, body(): pl.pallas_call(functools.partial(apply_kernel, float(cells) ** 0.5), grid...  3.54 us

profile of v2, /device:TPU:0, one launch (start us, length us, event | category | flops | bytes accessed | tf_op | source)
XLA Modules:
  0.0 42.5 jit_solution(4573195355827283460)
XLA Ops:
  0.6 38.4 %transport.1 = (f32[8,4,64,128]{3,2,1,0:T(8,128)}, f32[8,128]{1,0:T(8,128)}) custom-call(f32[8,4,64,128]{3,2,1,0:T(8,128)} %probes.1, f32[2,4,64,128]{3,2,1,0:T(8,128)} %wind.1, f32[2,4,64,128]{3,2,1,0:T(8,128)} %tend.1, f32[1,4,64,128]{3,2,1,0:T(8,128)} %bitcast.1), custom_call_target="tpu_custom_call" | custom-call | tf_op jit(solution)/shard_map/transport/pallas_call | solution.py:353
  39.0 3.5 %orthonormal.1 = (f32[8,4,64,128]{3,2,1,0:T(8,128)}, f32[8,8]{1,0:T(8,128)}) custom-call(f32[8,128]{1,0:T(8,128)} %get-tuple-element.4.inverse.tile, f32[8,128]{1,0:T(8,128)} %get-tuple-element.4.inverse.tile, f32[8,4,64,128]{3,2,1,0:T(8,128)} %get-tuple-element.5.z), custom_call_target="tpu_custom_call" | custom-call | tf_op jit(solution)/shard_map/orthonormal/pallas_call | solution.py:392

commit v3 on v2

--- a/solution.py
+++ b/solution.py
@@ -12,7 +12,6 @@
 MESH = pl.DeviceIdType.MESH
 
 HALO = 2 * STEPS
-OWN = 2 * HALO
 WINDOW = 32
 
 
@@ -24,7 +23,7 @@
 
 def transport_kernel(
     n_lat, n_lon, probes, wind, tend, weight, z_out, tile_out,
-    field, other, masks, z_buf, send_pack, recv_pack, sums, part,
+    field, stages, masks, z_buf, send_pack, recv_pack, sums, part,
     load_sem, z_sem, lon_send, lon_recv, lat_send, lat_recv,
     sum_send, sum_recv, part_send, part_recv,
 ):
@@ -55,7 +54,7 @@
     loads = [
         pltpu.make_async_copy(
             source,
-            field.at[pl.ds(first, size), pl.ds(0, levels), pl.ds(OWN, rows), :],
+            field.at[pl.ds(first, size), pl.ds(0, levels), pl.ds(HALO, rows), :],
             load_sem.at[k],
         )
         for k, (source, first, size) in enumerate(placed)
@@ -64,21 +63,16 @@
         load.start()
 
     zero = jnp.zeros((8, width), jnp.float32)
-    for buffer, size in ((field, entities), (other, count)):
-        for start in (0, OWN + rows + HALO):
-            buffer[:, :, pl.ds(start, 8), :] = jnp.zeros((size, levels + 2, 8, width), jnp.float32)
     total = width * n_lat
-    for level in range(levels):
-        masks[level] = jnp.ones((8, width), jnp.float32)
     for side, first in ((0, -HALO), (1, width - WINDOW + HALO)):
         column = lat * width + first + in_window
-        masks[levels + side] = jnp.where((column >= 0) & (column < total), 1.0, 0.0)
+        masks[side] = jnp.where((column >= 0) & (column < total), 1.0, 0.0)
 
     pl.semaphore_wait(barrier, n_lon + n_lat + 2)
 
     lon_copies = []
     for d, (to_lon, src_row, dst_row) in enumerate(
-        ((up_lon, rows - HALO, HALO), (down_lon, 0, OWN + rows))
+        ((up_lon, rows - HALO, 0), (down_lon, 0, HALO + rows))
     ):
         for k, (source, first, size) in enumerate(placed):
             copy = pltpu.make_async_remote_copy(
@@ -105,7 +99,7 @@
         load.wait()
 
     def pack(group, carry):
-        start = pl.multiple_of(OWN + 8 * group, 8)
+        start = pl.multiple_of(HALO + 8 * group, 8)
         to = pl.multiple_of(8 * group, 8)
         for side in range(2):
             packed = [zero] * ((entities + 3) // 4)
@@ -150,10 +144,80 @@
             for copy in lat_copies[side]:
                 copy.start()
 
+    groups = rows // 8 + 2
+    buffers = [field] + [stages.at[k] for k in range(2 * STEPS)]
+
+    def above(ref, lead, start, closed):
+        if closed:
+            return pltpu.roll(ref[(*lead, pl.ds(start, 8), slice(None))], 1, 0)
+        return ref[(*lead, pl.ds(start - 1, 8), slice(None))]
+
+    def below(ref, lead, start, closed):
+        if closed:
+            return pltpu.roll(ref[(*lead, pl.ds(start, 8), slice(None))], 7, 0)
+        return ref[(*lead, pl.ds(start + 1, 8), slice(None))]
+
+    def same(ref, lead, start, closed):
+        return ref[(*lead, pl.ds(start, 8), slice(None))]
+
+    def rate(which, step, level, start, read=same, closed=False):
+        now = read(field, (count + which, level), start, closed)
+        if step:
+            now = now + step * read(field, (count + 2 + which, level), start, closed)
+        return 0.5 * now
+
+    def run_step(number, first_level, last_level, chosen, top, bottom, unroll):
+        source, target = buffers[number], buffers[number + 1]
+        adjoint = number >= STEPS
+        step = 2 * STEPS - 1 - number if adjoint else number
+
+        def body(level, carry):
+            for group in chosen:
+                start = 8 * group
+                if adjoint:
+                    north = rate(1, step, level, start)
+                    before = DIFFUSE - rate(0, step, level, start, above, group == top)
+                    after = DIFFUSE + rate(0, step, level, start, below, group == bottom)
+                    left = pltpu.roll(DIFFUSE - north, 1, 1)
+                    right = pltpu.roll(DIFFUSE + north, width - 1, 1)
+                else:
+                    east = rate(0, step, level, start)
+                    north = rate(1, step, level, start)
+                    after = DIFFUSE - east
+                    before = DIFFUSE + east
+                    right = DIFFUSE - north
+                    left = DIFFUSE + north
+                centre = CENTRE
+                scale = None
+                if first_level >= levels:
+                    scale = masks[level - levels]
+                if number == STEPS - 1:
+                    seen = field[count + 4, level, pl.ds(start, 8), :]
+                    scale = seen if scale is None else scale * seen
+                if scale is not None:
+                    centre, before, after, left, right = (
+                        scale * x for x in (centre, before, after, left, right)
+                    )
+                for probe in range(count):
+                    lead = (probe, level)
+                    middle = source[probe, level, pl.ds(start, 8), :]
+                    target[probe, level, pl.ds(start, 8), :] = (
+                        (centre * middle + after * below(source, lead, start, group == bottom))
+                        + (before * above(source, lead, start, group == top)
+                           + right * pltpu.roll(middle, width - 1, 1))
+                        + left * pltpu.roll(middle, 1, 1)
+                    )
+            return carry
+
+        lax.fori_loop(first_level, last_level, body, 0, unroll=unroll)
+
+    for number in range(2 * STEPS):
+        run_step(number, 0, levels, range(1, groups - 1), 1, groups - 2, 1)
+
     for copy in lon_copies:
         copy.wait_recv()
 
-    for start in (HALO, OWN + rows):
+    for start in (0, HALO + rows):
         for entity in range(entities):
             for side in range(2):
                 field[entity, levels + side, pl.ds(start, 8), :] = own_window(entity, side, start)
@@ -169,7 +233,6 @@
             recv_pack[side] = jnp.zeros(recv_pack.shape[1:], jnp.float32)
 
     def unpack(group, carry):
-        start = pl.multiple_of(HALO + 8 * group, 8)
         at = pl.multiple_of(8 * group, 8)
         for side in range(2):
             here = in_window < 8 if side == 0 else in_window >= 24
@@ -177,67 +240,25 @@
                 slot = entity % 4
                 got = recv_pack[side, entity // 4, pl.ds(at, 8), :]
                 moved = pltpu.roll(got, ((0 if side == 0 else 24) - 8 * slot) % width, 1)
-                held = field[entity, levels + side, pl.ds(start, 8), :]
-                field[entity, levels + side, pl.ds(start, 8), :] = jnp.where(here, moved, held)
+                held = field[entity, levels + side, pl.ds(at, 8), :]
+                field[entity, levels + side, pl.ds(at, 8), :] = jnp.where(here, moved, held)
         return carry
 
-    groups = rows // 8 + 2
     lax.fori_loop(0, groups, unpack, 0, unroll=2)
 
-    def rate(which, step, level, start):
-        now = field[count + which, level, pl.ds(start, 8), :]
-        if step:
-            now = now + step * field[count + 2 + which, level, pl.ds(start, 8), :]
-        return 0.5 * now
-
-    def run_step(source, target, step, adjoint, first, last):
-        def body(level, carry):
-            edge = masks[level]
-            for group in range(first, last):
-                start = HALO + 8 * group
-                mask = edge
-                if adjoint:
-                    north = rate(1, step, level, start)
-                    before = mask * (DIFFUSE - rate(0, step, level, start - 1))
-                    after = mask * (DIFFUSE + rate(0, step, level, start + 1))
-                    left = mask * pltpu.roll(DIFFUSE - north, 1, 1)
-                    right = mask * pltpu.roll(DIFFUSE + north, width - 1, 1)
-                else:
-                    if step == STEPS - 1:
-                        mask = mask * field[count + 4, level, pl.ds(start, 8), :]
-                    east = rate(0, step, level, start)
-                    north = rate(1, step, level, start)
-                    after = mask * (DIFFUSE - east)
-                    before = mask * (DIFFUSE + east)
-                    right = mask * (DIFFUSE - north)
-                    left = mask * (DIFFUSE + north)
-                centre = CENTRE * mask
-                for probe in range(count):
-                    middle = source[probe, level, pl.ds(start, 8), :]
-                    target[probe, level, pl.ds(start, 8), :] = (
-                        (centre * middle + after * source[probe, level, pl.ds(start + 1, 8), :])
-                        + (before * source[probe, level, pl.ds(start - 1, 8), :]
-                           + right * pltpu.roll(middle, width - 1, 1))
-                        + left * pltpu.roll(middle, 1, 1)
-                    )
-            return carry
-
-        lax.fori_loop(0, levels + 2, body, 0)
-
-    source, target = field, other
-    for step in range(STEPS):
-        run_step(source, target, step, False, 0, groups)
-        source, target = target, source
-    for step in reversed(range(STEPS)):
-        run_step(source, target, step, True, int(step == 0), groups - int(step == 0))
-        source, target = target, source
+    for number in range(2 * STEPS):
+        last = int(number == 2 * STEPS - 1)
+        outer = (1, groups - 2) if last else (0, 1, groups - 2, groups - 1)
+        run_step(number, 0, levels, outer, 0, groups - 1, 2)
+        run_step(number, levels, levels + 2, range(last, groups - last), 0, groups - 1, 1)
+    source = buffers[-1]
 
     pairs = [(p, q) for p in range(count) for q in range(p, count)]
 
     accs = [zero] * len(pairs)
     for level in range(levels):
         def gather(group, accs):
-            start = pl.multiple_of(OWN + 8 * group, 8)
+            start = pl.multiple_of(HALO + 8 * group, 8)
             to = pl.multiple_of(8 * group, 8)
             values = []
             for probe in range(count):
@@ -348,7 +369,7 @@
     count, levels, rows, width = probes.shape
     entities = count + 5
     packs = (entities + 3) // 4
-    tall = rows + 4 * HALO
+    tall = rows + 2 * HALO
     f32 = jnp.float32
     z, tile = pl.pallas_call(
         functools.partial(transport_kernel, n_lat, n_lon),
@@ -363,8 +384,8 @@
         ),
         scratch_shapes=[
             pltpu.VMEM((entities, levels + 2, tall, width), f32),
-            pltpu.VMEM((count, levels + 2, tall, width), f32),
-            pltpu.VMEM((levels + 2, 8, width), f32),
+            pltpu.VMEM((2 * STEPS, count, levels + 2, tall, width), f32),
+            pltpu.VMEM((2, 8, width), f32),
             pltpu.VMEM(probes.shape, f32),
             pltpu.VMEM((2, packs, rows, width), f32),
             pltpu.VMEM((2, packs, rows + 2 * HALO, width), f32),

time: 42.7 us -> 38.1 us (0.89)
  Pallas kernels: 41.9 us -> 37.3 us
    pallas_call x1, Pallas kernels: 38.4 us -> 33.8 us  [body(): pl.pallas_call(functools.partial(transport_kernel, n_lat, n_lon), out_sha...]
where the time goes in v3:
time: 38.1 us; the launch traced here: 38 us
  Pallas kernels  37.3 us (98%)
  between operations  0.64 us (2%)
    pallas_call x1, Pallas kernels, body(): pl.pallas_call(functools.partial(transport_kernel, n_lat, n_lon), out_sha...  33.8 us
    pallas_call x1, Pallas kernels, body(): pl.pallas_call(functools.partial(apply_kernel, float(cells) ** 0.5), grid...  3.54 us

profile of v3, /device:TPU:0, one launch (start us, length us, event | category | flops | bytes accessed | tf_op | source)
XLA Modules:
  0.0 38.0 jit_solution(6035819274039395458)
XLA Ops:
  0.6 33.8 %transport.1 = (f32[8,4,64,128]{3,2,1,0:T(8,128)}, f32[8,128]{1,0:T(8,128)}) custom-call(f32[8,4,64,128]{3,2,1,0:T(8,128)} %probes.1, f32[2,4,64,128]{3,2,1,0:T(8,128)} %wind.1, f32[2,4,64,128]{3,2,1,0:T(8,128)} %tend.1, f32[1,4,64,128]{3,2,1,0:T(8,128)} %bitcast.1), custom_call_target="tpu_custom_call" | custom-call | tf_op jit(solution)/shard_map/transport/pallas_call | solution.py:374
  34.4 3.5 %orthonormal.1 = (f32[8,4,64,128]{3,2,1,0:T(8,128)}, f32[8,8]{1,0:T(8,128)}) custom-call(f32[8,128]{1,0:T(8,128)} %get-tuple-element.4.inverse.tile, f32[8,128]{1,0:T(8,128)} %get-tuple-element.4.inverse.tile, f32[8,4,64,128]{3,2,1,0:T(8,128)} %get-tuple-element.5.z), custom_call_target="tpu_custom_call" | custom-call | tf_op jit(solution)/shard_map/orthonormal/pallas_call | solution.py:413

commit v4 on v3

--- a/solution.py
+++ b/solution.py
@@ -115,7 +115,7 @@
                 send_pack[side, k, pl.ds(to, 8), :] = value
         return carry
 
-    lax.fori_loop(0, rows // 8, pack, 0)
+    lax.fori_loop(0, rows // 8, pack, 0, unroll=2)
 
     has = (lat > 0, lat < n_lat - 1)
     lat_copies = ([], [])
@@ -212,7 +212,7 @@
         lax.fori_loop(first_level, last_level, body, 0, unroll=unroll)
 
     for number in range(2 * STEPS):
-        run_step(number, 0, levels, range(1, groups - 1), 1, groups - 2, 1)
+        run_step(number, 0, levels, range(1, groups - 1), 1, groups - 2, 2)
 
     for copy in lon_copies:
         copy.wait_recv()
@@ -244,13 +244,13 @@
                 field[entity, levels + side, pl.ds(at, 8), :] = jnp.where(here, moved, held)
         return carry
 
-    lax.fori_loop(0, groups, unpack, 0, unroll=2)
+    lax.fori_loop(0, groups, unpack, 0, unroll=5)
 
     for number in range(2 * STEPS):
         last = int(number == 2 * STEPS - 1)
         outer = (1, groups - 2) if last else (0, 1, groups - 2, groups - 1)
-        run_step(number, 0, levels, outer, 0, groups - 1, 2)
-        run_step(number, levels, levels + 2, range(last, groups - last), 0, groups - 1, 1)
+        run_step(number, 0, levels, outer, 0, groups - 1, levels)
+        run_step(number, levels, levels + 2, range(last, groups - last), 0, groups - 1, 2)
     source = buffers[-1]
 
     pairs = [(p, q) for p in range(count) for q in range(p, count)]
@@ -347,22 +347,42 @@
     z_copy.wait()
 
 
-def apply_kernel(scale, inverse, tile, z, basis, factor):
-    count, _, rows, width = z.shape
+def apply_kernel(scale, tile, z, basis, factor, tile_buf, z_buf, out_buf, tile_sem, in_sem, out_sem):
+    count, levels, rows, width = z.shape
+    first = pltpu.make_async_copy(tile, tile_buf, tile_sem)
+    first.start()
+    loads = [
+        pltpu.make_async_copy(z.at[:, level], z_buf.at[:, level], in_sem.at[level])
+        for level in range(levels)
+    ]
+    for load in loads:
+        load.start()
+    first.wait()
+    found = tile_buf[...]
+    factor[...] = found[:, :count] * (1.0 / scale)
+    found = found * scale
     coefficients = [
-        [inverse[p, count + q] * scale for q in range(p + 1)] for p in range(count)
+        [
+            jnp.broadcast_to(found[p : p + 1, count + q : count + q + 1], (8, width))
+            for q in range(p + 1)
+        ]
+        for p in range(count)
     ]
-    for start in range(0, rows, 8):
-        values = [z[q, 0, pl.ds(start, 8), :] for q in range(count)]
-        for p in range(count):
-            total = coefficients[p][0] * values[0]
-            for q in range(1, p + 1):
-                total = total + coefficients[p][q] * values[q]
-            basis[p, 0, pl.ds(start, 8), :] = total
-
-    @pl.when(pl.program_id(0) == 0)
-    def _():
-        factor[...] = tile[:, :count] * (1.0 / scale)
+    stores = []
+    for level in range(levels):
+        loads[level].wait()
+        for start in range(0, rows, 8):
+            values = [z_buf[q, level, pl.ds(start, 8), :] for q in range(count)]
+            for p in range(count):
+                total = coefficients[p][0] * values[0]
+                for q in range(1, p + 1):
+                    total = total + coefficients[p][q] * values[q]
+                out_buf[p, level, pl.ds(start, 8), :] = total
+        store = pltpu.make_async_copy(out_buf.at[:, level], basis.at[:, level], out_sem.at[level])
+        store.start()
+        stores.append(store)
+    for store in stores:
+        store.wait()
 
 
 def body(probes, wind, wind_tend, obs_weight, *, n_lat, n_lon):
@@ -409,23 +429,28 @@
     )(probes, wind, wind_tend, obs_weight[None])
 
     cells = levels * rows * width * n_lat * n_lon
-    block = pl.BlockSpec((count, 1, rows, width), lambda level: (0, level, 0, 0))
     basis, factor = pl.pallas_call(
         functools.partial(apply_kernel, float(cells) ** 0.5),
-        grid=(levels,),
         out_shape=(
             jax.ShapeDtypeStruct(probes.shape, f32),
             jax.ShapeDtypeStruct((count, count), f32),
         ),
-        in_specs=[
-            pl.BlockSpec(memory_space=pltpu.SMEM),
-            pl.BlockSpec((8, width), lambda level: (0, 0)),
-            block,
+        in_specs=[pl.BlockSpec(memory_space=pltpu.HBM)] * 2,
+        out_specs=(
+            pl.BlockSpec(memory_space=pltpu.HBM),
+            pl.BlockSpec(memory_space=pltpu.VMEM),
+        ),
+        scratch_shapes=[
+            pltpu.VMEM((8, width), f32),
+            pltpu.VMEM(probes.shape, f32),
+            pltpu.VMEM(probes.shape, f32),
+            pltpu.SemaphoreType.DMA,
+            pltpu.SemaphoreType.DMA((levels,)),
+            pltpu.SemaphoreType.DMA((levels,)),
         ],
-        out_specs=(block, pl.BlockSpec((count, count), lambda level: (0, 0))),
         compiler_params=pltpu.CompilerParams(vmem_limit_bytes=60 * 2**20),
         name="orthonormal",
-    )(tile, tile, z)
+    )(tile, z)
     return basis, factor
 
 

time: 38.1 us -> 38.9 us (1.021)
  Pallas kernels: 37.3 us -> 38.2 us
    pallas_call x1, Pallas kernels: 33.8 us -> 35.4 us  [body(): pl.pallas_call(functools.partial(transport_kernel, n_lat, n_lon), out_sha...]
    pallas_call x1, Pallas kernels: 3.54 us -> 2.77 us  [body(): pl.pallas_call(functools.partial(apply_kernel, float(cells) ** 0.5), out_...]
where the time goes in v4:
time: 38.9 us; the launch traced here: 38.8 us
  Pallas kernels  38.2 us (98%)
  between operations  0.64 us (2%)
    pallas_call x1, Pallas kernels, body(): pl.pallas_call(functools.partial(transport_kernel, n_lat, n_lon), out_sha...  35.4 us
    pallas_call x1, Pallas kernels, body(): pl.pallas_call(functools.partial(apply_kernel, float(cells) ** 0.5), out_...  2.77 us

profile of v4, /device:TPU:0, one launch (start us, length us, event | category | flops | bytes accessed | tf_op | source)
XLA Modules:
  0.0 38.8 jit_solution(1512667232746565674)
XLA Ops:
  0.6 35.4 %transport.1 = (f32[8,4,64,128]{3,2,1,0:T(8,128)}, f32[8,128]{1,0:T(8,128)}) custom-call(f32[8,4,64,128]{3,2,1,0:T(8,128)} %probes.1, f32[2,4,64,128]{3,2,1,0:T(8,128)} %wind.1, f32[2,4,64,128]{3,2,1,0:T(8,128)} %tend.1, f32[1,4,64,128]{3,2,1,0:T(8,128)} %bitcast.1), custom_call_target="tpu_custom_call" | custom-call | tf_op jit(solution)/shard_map/transport/pallas_call | solution.py:394
  36.0 2.8 %orthonormal.1 = (f32[8,4,64,128]{3,2,1,0:T(8,128)}, f32[8,8]{1,0:T(8,128)}) custom-call(f32[8,128]{1,0:T(8,128)} %get-tuple-element.4.tile, f32[8,4,64,128]{3,2,1,0:T(8,128)} %get-tuple-element.5.z), custom_call_target="tpu_custom_call" | custom-call | tf_op jit(solution)/shard_map/orthonormal/pallas_call | solution.py:432

commit v5 on v4

--- a/solution.py
+++ b/solution.py
@@ -115,7 +115,7 @@
                 send_pack[side, k, pl.ds(to, 8), :] = value
         return carry
 
-    lax.fori_loop(0, rows // 8, pack, 0, unroll=2)
+    lax.fori_loop(0, rows // 8, pack, 0)
 
     has = (lat > 0, lat < n_lat - 1)
     lat_copies = ([], [])
@@ -212,7 +212,7 @@
         lax.fori_loop(first_level, last_level, body, 0, unroll=unroll)
 
     for number in range(2 * STEPS):
-        run_step(number, 0, levels, range(1, groups - 1), 1, groups - 2, 2)
+        run_step(number, 0, levels, range(1, groups - 1), 1, groups - 2, 1)
 
     for copy in lon_copies:
         copy.wait_recv()
@@ -244,13 +244,13 @@
                 field[entity, levels + side, pl.ds(at, 8), :] = jnp.where(here, moved, held)
         return carry
 
-    lax.fori_loop(0, groups, unpack, 0, unroll=5)
+    lax.fori_loop(0, groups, unpack, 0, unroll=2)
 
     for number in range(2 * STEPS):
         last = int(number == 2 * STEPS - 1)
         outer = (1, groups - 2) if last else (0, 1, groups - 2, groups - 1)
-        run_step(number, 0, levels, outer, 0, groups - 1, levels)
-        run_step(number, levels, levels + 2, range(last, groups - last), 0, groups - 1, 2)
+        run_step(number, 0, levels, outer, 0, groups - 1, 2)
+        run_step(number, levels, levels + 2, range(last, groups - last), 0, groups - 1, 1)
     source = buffers[-1]
 
     pairs = [(p, q) for p in range(count) for q in range(p, count)]

time: 38.9 us -> 37.3 us (0.959)
  Pallas kernels: 38.2 us -> 36.6 us
    pallas_call x1, Pallas kernels: 35.4 us -> 33.8 us  [body(): pl.pallas_call(functools.partial(transport_kernel, n_lat, n_lon), out_sha...]
where the time goes in v5:
time: 37.3 us; the launch traced here: 37.2 us
  Pallas kernels  36.6 us (98%)
  between operations  0.64 us (2%)
    pallas_call x1, Pallas kernels, body(): pl.pallas_call(functools.partial(transport_kernel, n_lat, n_lon), out_sha...  33.8 us
    pallas_call x1, Pallas kernels, body(): pl.pallas_call(functools.partial(apply_kernel, float(cells) ** 0.5), out_...  2.77 us

profile of v5, /device:TPU:0, one launch (start us, length us, event | category | flops | bytes accessed | tf_op | source)
XLA Modules:
  0.0 37.2 jit_solution(1626590292157459703)
XLA Ops:
  0.6 33.8 %transport.1 = (f32[8,4,64,128]{3,2,1,0:T(8,128)}, f32[8,128]{1,0:T(8,128)}) custom-call(f32[8,4,64,128]{3,2,1,0:T(8,128)} %probes.1, f32[2,4,64,128]{3,2,1,0:T(8,128)} %wind.1, f32[2,4,64,128]{3,2,1,0:T(8,128)} %tend.1, f32[1,4,64,128]{3,2,1,0:T(8,128)} %bitcast.1), custom_call_target="tpu_custom_call" | custom-call | tf_op jit(solution)/shard_map/transport/pallas_call | solution.py:394
  34.4 2.8 %orthonormal.1 = (f32[8,4,64,128]{3,2,1,0:T(8,128)}, f32[8,8]{1,0:T(8,128)}) custom-call(f32[8,128]{1,0:T(8,128)} %get-tuple-element.4.tile, f32[8,4,64,128]{3,2,1,0:T(8,128)} %get-tuple-element.5.z), custom_call_target="tpu_custom_call" | custom-call | tf_op jit(solution)/shard_map/orthonormal/pallas_call | solution.py:432
